TPU v7x, 32 devices: a whole 2x2x4 slice. The times are simulated.
32 devices in a mesh: grp: 8 (over z, y), dp: 4 (over x, core).
Axes of the slice: x: 2, y: 2, z: 4, core: 2. Of those that a mesh axis runs over, the one named last changes fastest.
Arguments:
- tokens: bfloat16 [32, 256, 768], P(('grp', 'dp')), may hold values from -6 to 6
- condition: bfloat16 [32, 768], P(('grp', 'dp')), may hold values from -6 to 6
- bucket: int32 [32], P(('grp', 'dp')), may hold values from 0 to 63, as said below
- live_mask: int32 [32], P(('grp', 'dp')), may hold values from 0 to 1, as said below
- routes: int32 [32, 256, 2], P(('grp', 'dp')), may hold values from 0 to 3, all different within a row; in each aligned block of 256 rows (0 to 255, 256 to 511, ..., all dimensions but the last counted through in order) at most 256 rows name the same one
- bucket_table: bfloat16 [64, 768], replicated, may hold values from -6 to 6
- ada_weight: bfloat16 [768, 4608], replicated, may hold values from -0.21875 to 0.21875
- ada_bias: bfloat16 [4608], replicated, may hold values from -3 to 3
- qkv_weight: bfloat16 [768, 2304], replicated, may hold values from -0.21875 to 0.21875
- proj_weight: bfloat16 [768, 768], replicated, may hold values from -0.875 to 0.875
- shared_up: bfloat16 [768, 3072], replicated, may hold values from -0.21875 to 0.21875
- shared_down: bfloat16 [3072, 768], replicated, may hold values from -0.109375 to 0.109375
- router_weight: bfloat16 [768, 4], replicated, may hold values from -0.21875 to 0.21875
- expert_up: bfloat16 [4, 768, 3072], P('dp'), may hold values from -0.21875 to 0.21875
- expert_down: bfloat16 [4, 3072, 768], P('dp'), may hold values from -0.109375 to 0.109375
- cotangent: bfloat16 [32, 256, 768], P(('grp', 'dp')), may hold values from -6 to 6
Outputs:
- mixed_out: bfloat16 [32, 256, 768], P(('grp', 'dp'))
- grad_tokens: float32 [32, 256, 768], P(('grp', 'dp'))
- grad_condition: float32 [32, 768], P(('grp', 'dp'))
- grad_table: float32 [64, 768], P('grp')
- grad_ada_weight: float32 [768, 4608], P('grp')
- grad_ada_bias: float32 [4608], P('grp')
- grad_qkv: float32 [768, 2304], P('grp')
- grad_proj: float32 [768, 768], P('grp')
- grad_shared_up: float32 [768, 3072], P('grp')
- grad_shared_down: float32 [3072, 768], P('grp')
- grad_router: float32 [768, 4], P('grp')
- grad_expert_up: float32 [4, 768, 3072], P('dp', 'grp')
- grad_expert_down: float32 [4, 3072, 768], P('dp', 'grp')
Inputs may be any that keep to these rules, and one draw needn't show every extreme that they name: `routes`: in the rows of one device (256 patches in order) each patch names 2 different experts, no expert is named by more than 256 of them. An image of group g (slots g * 4 to g * 4 + 3) has a bucket from g * 8 to g * 8 + 7; lower buckets of a group are more common. `live_mask`: in each group of 4 slots the live images come first; every group holds one or more, the first group is full, and no group holds more than the one before it.
All inputs are finite; a program needn't handle non-finite values.
Results may differ from a plain program's by a relative error of at most 0.024.
Values may be sent and summed in bfloat16 or wider, within the bound.
No kernel may reach another device: no remote copies, remote signals or barrier semaphores. Data moves between devices by JAX's collectives and lax.ppermute only.
A program may use at most 192 MiB of HBM per device.

v0:
```python
import jax
import jax.numpy as jnp
from jax import lax
from jax.sharding import PartitionSpec as P

HEADS = 12
TOP = 2


EPSILON = 1e-06


def product(left_mat, right_mat):
    return jnp.dot(left_mat, right_mat, preferred_element_type=jnp.float32)


def product_tn(left_mat, right_mat):
    return lax.dot_general(
        left_mat, right_mat, (((0,), (0,)), ((), ())), preferred_element_type=jnp.float32
    )


def product_nt(left_mat, right_mat):
    return lax.dot_general(
        left_mat, right_mat, (((1,), (1,)), ((), ())), preferred_element_type=jnp.float32
    )


def to_low(tensor):
    return tensor.astype(jnp.bfloat16)


def normalize(tensor):
    average = jnp.mean(tensor, axis=-1, keepdims=True)
    centered = tensor - average
    inverse = lax.rsqrt(jnp.mean(centered * centered, axis=-1, keepdims=True) + EPSILON)
    return (centered * inverse, inverse)


def normalize_back(gradient, normed, inverse):
    first_term = jnp.mean(gradient, axis=-1, keepdims=True)
    second_term = jnp.mean(gradient * normed, axis=-1, keepdims=True)
    return inverse * (gradient - first_term - normed * second_term)


def local_back(function, tensor, gradient):
    return jax.vjp(function, tensor)[1](gradient)[0]


def per_device(
    tokens,
    condition,
    bucket,
    live_mask,
    routes,
    bucket_table,
    ada_weight,
    ada_bias,
    qkv_weight,
    proj_weight,
    shared_up,
    shared_down,
    router_weight,
    expert_up,
    expert_down,
    cotangent,
):
    image_count, patch_count, model_width = tokens.shape
    row_count = image_count * patch_count
    head_size = model_width // HEADS
    scaling = float(head_size) ** (-0.5)
    member_count = lax.axis_size("dp")
    expert_count = expert_up.shape[0] * member_count
    slot_count = 2 * TOP * row_count // expert_count
    table_rows = bucket_table.shape[0]
    inputs = tokens.astype(jnp.float32)
    selector = (bucket[:, None] == jnp.arange(table_rows, dtype=jnp.int32)[None, :]).astype(
        jnp.float32
    )
    conditioned = condition.astype(jnp.float32) + jnp.dot(
        selector, bucket_table.astype(jnp.float32), precision=lax.Precision.HIGHEST
    )
    activated = to_low(jax.nn.silu(conditioned))
    modulation = product(activated, ada_weight) + ada_bias.astype(jnp.float32)
    pieces = modulation.reshape(image_count, 6, 1, model_width)
    shift_attn, scale_attn, gate_attn, shift_mix, scale_mix, gate_mix = [
        pieces[:, number] for number in range(6)
    ]
    normed_one, inverse_one = normalize(inputs)
    attn_in = to_low(normed_one * (1.0 + scale_attn) + shift_attn).reshape(row_count, model_width)
    projected = to_low(product(attn_in, qkv_weight)).reshape(
        image_count, patch_count, 3, HEADS, head_size
    )
    query_rows = projected[:, :, 0]
    key_rows = projected[:, :, 1]
    value_rows = projected[:, :, 2]
    scores = (
        jnp.einsum("bqhd,bkhd->bhqk", query_rows, key_rows, preferred_element_type=jnp.float32)
        * scaling
    )
    top_score = jnp.max(scores, axis=-1, keepdims=True)
    weights_exp = jnp.exp(scores - top_score)
    totals = jnp.sum(weights_exp, axis=-1, keepdims=True)
    log_total = top_score + jnp.log(totals)
    probs_first = to_low(weights_exp / totals)
    attended = jnp.einsum(
        "bhqk,bkhd->bqhd", probs_first, value_rows, preferred_element_type=jnp.float32
    )
    attended = to_low(attended.reshape(row_count, model_width))
    attn_out = product(attended, proj_weight).reshape(image_count, patch_count, model_width)
    middle = inputs + gate_attn * attn_out
    normed_two, inverse_two = normalize(middle)
    mix_in = to_low(normed_two * (1.0 + scale_mix) + shift_mix).reshape(row_count, model_width)
    shared_pre = product(mix_in, shared_up)
    shared_act = to_low(jax.nn.gelu(shared_pre))
    shared_out = product(shared_act, shared_down)
    logits = product(mix_in, router_weight)
    expert_ids = jnp.arange(expert_count, dtype=jnp.int32)
    chosen_hot = (routes.reshape(row_count, TOP)[:, :, None] == expert_ids[None, None, :]).astype(
        jnp.float32
    )
    chosen = jnp.sum(logits[:, None, :] * chosen_hot, axis=-1)
    gate_vals = jax.nn.softmax(chosen, axis=-1)
    flat_routes = routes.reshape(row_count * TOP)
    route_hot = (flat_routes[:, None] == expert_ids[None, :]).astype(jnp.int32)
    places = jnp.sum(route_hot * (jnp.cumsum(route_hot, axis=0) - 1), axis=1)
    slot_index = flat_routes * slot_count + places
    outgoing = (
        jnp.zeros((expert_count * slot_count, model_width), jnp.bfloat16)
        .at[slot_index]
        .set(jnp.repeat(mix_in, TOP, axis=0))
    )
    arrived = lax.all_to_all(
        outgoing.reshape(member_count, -1, model_width),
        "dp",
        split_axis=0,
        concat_axis=0,
        tiled=True,
    )
    arrived = arrived.reshape(member_count, expert_up.shape[0], slot_count, model_width)
    expert_pre = jnp.einsum(
        "secw,ewf->secf", arrived, expert_up, preferred_element_type=jnp.float32
    )
    expert_act = to_low(jax.nn.gelu(expert_pre))
    expert_res = to_low(
        jnp.einsum("secf,efw->secw", expert_act, expert_down, preferred_element_type=jnp.float32)
    )
    returned = lax.all_to_all(
        expert_res.reshape(member_count, -1, model_width),
        "dp",
        split_axis=0,
        concat_axis=0,
        tiled=True,
    )
    routed = returned.reshape(expert_count * slot_count, model_width)[slot_index].reshape(
        row_count, TOP, model_width
    )
    routed_wide = routed.astype(jnp.float32)
    mixture = shared_out + jnp.sum(gate_vals[:, :, None] * routed_wide, axis=1)
    mixture = mixture.reshape(image_count, patch_count, model_width)
    alive_rows = live_mask.astype(jnp.float32)[:, None, None]
    result = (middle + gate_mix * mixture) * alive_rows
    mixed_out = result.astype(jnp.bfloat16)
    grad_result = cotangent.astype(jnp.float32) * alive_rows
    grad_gate_mix = jnp.sum(grad_result * mixture, axis=1)
    grad_mixture = (gate_mix * grad_result).reshape(row_count, model_width)
    grad_shared_out = to_low(grad_mixture)
    grad_shared_down = product_tn(shared_act, grad_shared_out)
    grad_shared_pre = to_low(
        local_back(jax.nn.gelu, shared_pre, product_nt(grad_shared_out, shared_down))
    )
    grad_shared_up = product_tn(mix_in, grad_shared_pre)
    grad_mix_in = product_nt(grad_shared_pre, shared_up)
    grad_routed = to_low(gate_vals[:, :, None] * grad_mixture[:, None, :])
    grad_gates = jnp.sum(grad_mixture[:, None, :] * routed_wide, axis=-1)
    grad_chosen = gate_vals * (grad_gates - jnp.sum(gate_vals * grad_gates, axis=-1, keepdims=True))
    grad_logits = to_low(jnp.sum(grad_chosen[:, :, None] * chosen_hot, axis=1))
    grad_router = product_tn(mix_in, grad_logits)
    grad_mix_in = grad_mix_in + product_nt(grad_logits, router_weight)
    grad_outgoing = (
        jnp.zeros((expert_count * slot_count, model_width), jnp.bfloat16)
        .at[slot_index]
        .set(grad_routed.reshape(row_count * TOP, model_width))
    )
    grad_arrived = lax.all_to_all(
        grad_outgoing.reshape(member_count, -1, model_width),
        "dp",
        split_axis=0,
        concat_axis=0,
        tiled=True,
    )
    grad_arrived = grad_arrived.reshape(member_count, expert_up.shape[0], slot_count, model_width)
    grad_down_local = jnp.einsum(
        "secf,secw->efw", expert_act, grad_arrived, preferred_element_type=jnp.float32
    )
    grad_expert_act = jnp.einsum(
        "secw,efw->secf", grad_arrived, expert_down, preferred_element_type=jnp.float32
    )
    grad_expert_pre = to_low(local_back(jax.nn.gelu, expert_pre, grad_expert_act))
    grad_up_local = jnp.einsum(
        "secw,secf->ewf", arrived, grad_expert_pre, preferred_element_type=jnp.float32
    )
    grad_sent = jnp.einsum(
        "secf,ewf->secw", grad_expert_pre, expert_up, preferred_element_type=jnp.float32
    )
    grad_back = lax.all_to_all(
        grad_sent.reshape(member_count, -1, model_width).astype(jnp.bfloat16),
        "dp",
        split_axis=0,
        concat_axis=0,
        tiled=True,
    ).astype(jnp.float32)
    grad_back = grad_back.reshape(expert_count * slot_count, model_width)[slot_index].reshape(
        row_count, TOP, model_width
    )
    grad_mix_in = (grad_mix_in + jnp.sum(grad_back, axis=1)).reshape(
        image_count, patch_count, model_width
    )
    grad_shift_mix = jnp.sum(grad_mix_in, axis=1)
    grad_scale_mix = jnp.sum(grad_mix_in * normed_two, axis=1)
    grad_middle = grad_result + normalize_back(
        grad_mix_in * (1.0 + scale_mix), normed_two, inverse_two
    )
    grad_gate_attn = jnp.sum(grad_middle * attn_out, axis=1)
    grad_attn_out = to_low((gate_attn * grad_middle).reshape(row_count, model_width))
    grad_proj = product_tn(attended, grad_attn_out)
    grad_attended = to_low(product_nt(grad_attn_out, proj_weight)).reshape(
        image_count, patch_count, HEADS, head_size
    )
    scores_again = (
        jnp.einsum("bqhd,bkhd->bhqk", query_rows, key_rows, preferred_element_type=jnp.float32)
        * scaling
    )
    probs_again = jnp.exp(scores_again - log_total)
    grad_probs = jnp.einsum(
        "bqhd,bkhd->bhqk", grad_attended, value_rows, preferred_element_type=jnp.float32
    )
    grad_value = jnp.einsum(
        "bhqk,bqhd->bkhd", to_low(probs_again), grad_attended, preferred_element_type=jnp.float32
    )
    grad_scores = to_low(
        probs_again * (grad_probs - jnp.sum(probs_again * grad_probs, axis=-1, keepdims=True))
    )
    grad_query = (
        jnp.einsum("bhqk,bkhd->bqhd", grad_scores, key_rows, preferred_element_type=jnp.float32)
        * scaling
    )
    grad_key = (
        jnp.einsum("bhqk,bqhd->bkhd", grad_scores, query_rows, preferred_element_type=jnp.float32)
        * scaling
    )
    grad_projected = to_low(
        jnp.stack([grad_query, grad_key, grad_value], axis=2).reshape(row_count, 3 * model_width)
    )
    grad_qkv = product_tn(attn_in, grad_projected)
    grad_attn_in = product_nt(grad_projected, qkv_weight).reshape(
        image_count, patch_count, model_width
    )
    grad_shift_attn = jnp.sum(grad_attn_in, axis=1)
    grad_scale_attn = jnp.sum(grad_attn_in * normed_one, axis=1)
    grad_tokens = grad_middle + normalize_back(
        grad_attn_in * (1.0 + scale_attn), normed_one, inverse_one
    )
    grad_modulation = jnp.concatenate(
        [
            grad_shift_attn,
            grad_scale_attn,
            grad_gate_attn,
            grad_shift_mix,
            grad_scale_mix,
            grad_gate_mix,
        ],
        axis=1,
    )
    grad_ada_bias = jnp.sum(grad_modulation, axis=0)
    grad_mod_low = to_low(grad_modulation)
    grad_ada_weight = product_tn(activated, grad_mod_low)
    grad_condition = local_back(jax.nn.silu, conditioned, product_nt(grad_mod_low, ada_weight))
    grad_table = jnp.dot(selector.T, grad_condition, precision=lax.Precision.HIGHEST)
    expert_up_grad = grad_up_local[0]
    expert_down_grad = grad_down_local[0]
    shares = (
        lax.psum_scatter(
            grad_table.astype(jnp.bfloat16), "grp", scatter_dimension=0, tiled=True
        ).astype(jnp.float32),
        lax.psum_scatter(
            grad_ada_weight.astype(jnp.bfloat16), "grp", scatter_dimension=0, tiled=True
        ).astype(jnp.float32),
        lax.psum_scatter(
            grad_ada_bias.astype(jnp.bfloat16), "grp", scatter_dimension=0, tiled=True
        ).astype(jnp.float32),
        lax.psum_scatter(
            grad_qkv.astype(jnp.bfloat16), "grp", scatter_dimension=0, tiled=True
        ).astype(jnp.float32),
        lax.psum_scatter(
            grad_proj.astype(jnp.bfloat16), "grp", scatter_dimension=0, tiled=True
        ).astype(jnp.float32),
        lax.psum_scatter(
            grad_shared_up.astype(jnp.bfloat16), "grp", scatter_dimension=0, tiled=True
        ).astype(jnp.float32),
        lax.psum_scatter(
            grad_shared_down.astype(jnp.bfloat16), "grp", scatter_dimension=0, tiled=True
        ).astype(jnp.float32),
        lax.psum_scatter(
            grad_router.astype(jnp.bfloat16), "grp", scatter_dimension=0, tiled=True
        ).astype(jnp.float32),
        lax.psum_scatter(
            expert_up_grad.astype(jnp.bfloat16), "grp", scatter_dimension=0, tiled=True
        ).astype(jnp.float32),
        lax.psum_scatter(
            expert_down_grad.astype(jnp.bfloat16), "grp", scatter_dimension=0, tiled=True
        ).astype(jnp.float32),
    )
    summed = (
        lax.psum(shares[0].astype(jnp.bfloat16), "dp").astype(jnp.float32),
        lax.psum(shares[1].astype(jnp.bfloat16), "dp").astype(jnp.float32),
        lax.psum(shares[2].astype(jnp.bfloat16), "dp").astype(jnp.float32),
        lax.psum(shares[3].astype(jnp.bfloat16), "dp").astype(jnp.float32),
        lax.psum(shares[4].astype(jnp.bfloat16), "dp").astype(jnp.float32),
        lax.psum(shares[5].astype(jnp.bfloat16), "dp").astype(jnp.float32),
        lax.psum(shares[6].astype(jnp.bfloat16), "dp").astype(jnp.float32),
        lax.psum(shares[7].astype(jnp.bfloat16), "dp").astype(jnp.float32),
    )
    table_part, ada_w_part, ada_b_part, qkv_part, proj_part, up_part, down_part, router_part = (
        summed
    )
    return (
        mixed_out,
        grad_tokens,
        grad_condition,
        table_part,
        ada_w_part,
        ada_b_part,
        qkv_part,
        proj_part,
        up_part,
        down_part,
        router_part,
        shares[8][None],
        shares[9][None],
    )


def solution(mesh):
    in_specs = (
        P(("grp", "dp"), None, None),
        P(("grp", "dp"), None),
        P(("grp", "dp")),
        P(("grp", "dp")),
        P(("grp", "dp"), None, None),
        P(),
        P(),
        P(),
        P(),
        P(),
        P(),
        P(),
        P(),
        P("dp", None, None),
        P("dp", None, None),
        P(("grp", "dp"), None, None),
    )
    out_specs = (
        P(("grp", "dp"), None, None),
        P(("grp", "dp"), None, None),
        P(("grp", "dp"), None),
        P("grp", None),
        P("grp", None),
        P("grp"),
        P("grp", None),
        P("grp", None),
        P("grp", None),
        P("grp", None),
        P("grp", None),
        P("dp", "grp", None),
        P("dp", "grp", None),
    )
    return jax.shard_map(
        per_device, mesh=mesh, in_specs=in_specs, out_specs=out_specs, check_vma=False
    )
```

profile of v0, /device:TPU:0, one launch (start us, length us, event | category | flops | bytes accessed | tf_op | source)
XLA Modules:
  0.0 1090.1 jit_solution(1732026457619207097)
XLA Ops:
  7.2 1.6 copy.85
  14.0 1.6 convert_reduce_fusion.1
  15.6 4.1 convolution_reduce_fusion
  26.1 3.2 convolution_convert_fusion.3
  29.3 2.4 copy.81
  31.6 1.7 multiply_reduce_fusion.1
  34.0 2.2 fusion.63
  40.8 3.0 reshape.692
  45.0 2.3 reduce-window.6
  54.7 4.4 scatter_custom_fusion
  59.0 4.6 all-to-all-start
  70.7 1.6 div.67
  74.3 1.7 mul.441
  75.9 3.2 mul.448
  79.1 4.7 scatter_custom_fusion.1
  83.8 3.9 fusion.140
  87.7 1.7 copy-done.54
  89.4 7.1 fusion.37
  96.5 4.3 all-to-all-start.2
  100.8 7.4 fusion.27
  108.2 4.6 copy-done.56
  112.7 10.8 fusion.40
  123.5 4.8 all-to-all-start.1
  128.3 15.3 %fusion.6 = bf16[4,1,256,3072]{3,2,0,1:T(8,128)(2,1)S(1)} fusion(f32[4,256,3072]{2,1,0:T(8,128)} %copy-done.56, bf16[4,256,768]{2,1,0:T(8,128)(2,1)} %all-to-all-done.2, bf16[1,3072,768]{2,1,0:T(8,128)(2,1)} %param.30), kind=kOutput, calls=%fused_computation.13 | convolution fusion | flops 4894752768 | bytes 25165824 | tf_op jit(solution)/shard_map/secw,efw->secf/dot_general | solution.py:196
  143.7 2.6 copy-done.55
  146.3 8.5 fusion.45
  154.8 4.4 all-to-all-start.3
  159.2 5.1 fusion.142
  164.4 5.0 gather_fusion
  169.4 3.0 reshape.666
  172.3 5.2 multiply_reduce_fusion.2
  181.1 3.3 bitcast_convert_fusion.2
  184.3 5.2 gather_fusion.1
  189.6 3.0 reshape.658
  192.6 4.2 reduce_sum.247
  196.8 2.9 fusion.80
  200.4 6.8 fusion.79
  210.6 2.8 convolution_convert_fusion.5
  213.4 1.9 copy.90
  215.3 3.2 multiply_reduce_fusion
  222.7 3.1 convolution_convert_fusion.2
  225.9 5.2 convolution_convert_fusion.1
  231.8 6.4 convolution_convert_fusion
  239.8 3.3 fusion.76
  249.8 5.0 multiply_convert_fusion
  258.1 5.5 fusion.136
  264.5 12.0 %bitcast_convert_fusion = bf16[3072,768]{1,0:T(8,128)(2,1)} fusion(bf16[4,256,768]{2,1,0:T(8,128)(2,1)} %all-to-all-done.2, f32[4,256,3072]{2,1,0:T(8,128)} %copy-done.56), kind=kOutput, calls=%fused_computation.21 | convolution fusion | flops 4862509056 | bytes 18874368 | tf_op jit(solution)/shard_map/secf,secw->efw/dot_general | solution.py:193
  276.6 9.1 bitcast_convert_fusion.1
  294.4 64.1 %reduce-scatter.16.cloned.1.call-done = bf16[96,2304]{1,0:T(8,128)(2,1)} async-done(((bf16[768,2304]{1,0:T(8,128)(2,1)}), bf16[96,2304]{1,0:T(8,128)(2,1)}) %reduce-scatter.16.cloned.1.call-update) | async-done | bytes 442384 | tf_op jit(solution)/shard_map/reduce_scatter | solution.py:292
  358.5 98.6 %reduce-scatter.20.cloned.1.call-done = bf16[96,3072]{1,0:T(8,128)(2,1)} async-done(((bf16[768,3072]{1,0:T(8,128)(2,1)}), bf16[96,3072]{1,0:T(8,128)(2,1)}) %reduce-scatter.20.cloned.1.call-update) | async-done | bytes 589840 | tf_op jit(solution)/shard_map/reduce_scatter | solution.py:298
  457.2 98.7 %reduce-scatter.22.cloned.1.call-done = bf16[384,768]{1,0:T(8,128)(2,1)} async-done(((bf16[3072,768]{1,0:T(8,128)(2,1)}), bf16[384,768]{1,0:T(8,128)(2,1)}) %reduce-scatter.22.cloned.1.call-update) | async-done | bytes 589840 | tf_op jit(solution)/shard_map/reduce_scatter | solution.py:301
  555.9 132.3 %reduce-scatter.14.cloned.1.call-done = bf16[96,4608]{1,0:T(8,128)(2,1)} async-done(((bf16[768,4608]{1,0:T(8,128)(2,1)}), bf16[96,4608]{1,0:T(8,128)(2,1)}) %reduce-scatter.14.cloned.1.call-update) | async-done | bytes 884752 | tf_op jit(solution)/shard_map/reduce_scatter | solution.py:286
  690.3 35.3 %all-reduce = bf16[4608]{0:T(1024)(128)(2,1)} all-reduce(bf16[4608]{0:T(1024)(128)(2,1)S(1)} %reduce.38), channel_id=4, replica_groups=mesh['grp'=8,'dp'=4] {'grp'}, use_global_device_ids=true, to_apply=%region_34.35.clone | all-reduce | flops 4608 | bytes 18432
  726.3 2.7 fusion.75
  729.0 23.5 %reduce-scatter.28.cloned.1.call-done = bf16[96,4]{1,0:T(8,128)(2,1)} async-done(((bf16[768,4]{1,0:T(8,128)(2,1)}), bf16[96,4]{1,0:T(8,128)(2,1)}) %reduce-scatter.28.cloned.1.call-update) | async-done | bytes 784
  753.9 59.4 %reduce-scatter.12.cloned.1.call-done = bf16[8,768]{1,0:T(8,128)(2,1)} async-done(((bf16[64,768]{1,0:T(8,128)(2,1)}), bf16[8,768]{1,0:T(8,128)(2,1)}) %reduce-scatter.12.cloned.1.call-update) | async-done | bytes 12304 | tf_op jit(solution)/shard_map/reduce_scatter | solution.py:283
  813.3 11.2 %all-reduce.1 = (bf16[8,768]{1,0:T(8,128)(2,1)S(1)}, bf16[576]{0:T(1024)(128)(2,1)}, bf16[96,4]{0,1:T(4,128)(2,1)}) all-reduce(bf16[8,768]{1,0:T(8,128)(2,1)} %reduce-scatter.12.cloned.1.call-done, bf16[576]{0:T(1024)(128)(2,1)S(1)} %dynamic-slice.1, bf16[96,4]{0,1:T(4,128)(2,1)} %copy.103), channel_id=1, replica_groups=mesh['grp'=8,'dp'=4] {'dp'}, use_global_device_ids=true, to_apply=%region_31.32 | all-reduce | flops 7104 | bytes 28416 | tf_op jit(solution)/shard_map/psum | solution.py:315
  827.7 84.2 %reduce-scatter.26.cloned.1.call-done = bf16[384,768]{1,0:T(8,128)(2,1)} async-done(((bf16[3072,768]{1,0:T(8,128)(2,1)}), bf16[384,768]{1,0:T(8,128)(2,1)}) %reduce-scatter.26.cloned.1.call-update) | async-done | bytes 589840 | tf_op jit(solution)/shard_map/reduce_scatter | solution.py:310
  911.9 2.2 bitcast_convert_fusion.3
  914.0 97.5 %reduce-scatter.24.cloned.1.call-done = bf16[96,3072]{1,0:T(8,128)(2,1)} async-done(((bf16[768,3072]{1,0:T(8,128)(2,1)}), bf16[96,3072]{1,0:T(8,128)(2,1)}) %reduce-scatter.24.cloned.1.call-update) | async-done | bytes 589840 | tf_op jit(solution)/shard_map/reduce_scatter | solution.py:307
  1011.5 2.2 bitcast_convert_fusion.4
  1013.7 61.5 %all-reduce.5.cloned.1.call-done = (bf16[96,4608]{1,0:T(8,128)(2,1)}, bf16[96,2304]{1,0:T(8,128)(2,1)}, bf16[96,768]{1,0:T(8,128)(2,1)}, bf16[96,3072]{1,0:T(8,128)(2,1)}, bf16[384,768]{1,0:T(8,128)(2,1)}) async-done(((bf16[96,4608]{1,0:T(8,128)(2,1)}, bf16[96,2304]{1,0:T(8,128)(2,1)}, bf16[96,768]{1,0:T(8,128)(2,1)}, bf16[96,3072]{1,0:T(8,128)(2,1)}, bf16[384,768]{1,0:T(8,128)(2,1)}), ...) | async-done | bytes 2654224 | tf_op jit(solution)/shard_map/psum | solution.py:316
  1075.2 2.6 convert_element_type.251
  1077.8 2.2 convert_element_type.259
  (215 shorter events, 76.0 us)
Async XLA Ops:
  7.2 18.9 %copy-start = (bf16[768,2304]{1,0:T(8,128)(2,1)S(1)}, bf16[768,2304]{1,0:T(8,128)(2,1)}, u32[]{:S(2)}) copy-start(bf16[768,2304]{1,0:T(8,128)(2,1)} %param.24) | copy-start | bytes 10616836
  15.6 4.1 copy-start.47
  15.6 4.1 copy-start.48
  15.6 4.1 copy-start.49
  23.1 2.4 copy-start.23
  23.1 2.4 copy-start.28
  23.1 184.1 %copy-start.30 = (f32[768]{0:T(1024)}, f32[768]{0:T(1024)S(1)}, u32[]{:S(2)}) copy-start(f32[768]{0:T(1024)S(1)} %get-tuple-element.28) | copy-start | bytes 9220
  24.2 1.3 copy-start.33
  33.4 2.8 copy-start.1
  33.4 2.8 copy-start.26
  34.0 2.2 copy-start.31
  34.0 2.2 copy-start.3
  34.0 2.2 copy-start.11
  36.2 1.7 copy-start.15
  37.9 5.8 copy-start.50
  50.8 14.6 %copy-start.32 = (s32[1,256,2]{1,2,0:T(2,128)S(1)}, s32[1,256,2]{1,2,0:T(2,128)}, u32[]{:S(2)}) copy-start(s32[1,256,2]{1,2,0:T(2,128)} %param.20) | copy-start | bytes 6148
  54.7 9.0 copy-start.52
  59.0 37.4 %all-to-all-start = ((bf16[4,256,768]{2,1,0:T(8,128)(2,1)}), bf16[4,256,768]{2,1,0:T(8,128)(2,1)}, u32[]{:S(2)}, u32[]{:S(2)}) async-start(bf16[4,256,768]{2,1,0:T(8,128)(2,1)} %bitcast.265), calls=%async_computation | async-start | bytes 3145728 | tf_op jit(solution)/shard_map/all_to_all | solution.py:133
  73.4 0.9 copy-start.10
  83.8 5.6 copy-start.21
  83.8 5.6 copy-start.43
  87.7 1.7 copy-start.54
  96.5 27.0 %all-to-all-start.2 = ((bf16[4,256,768]{2,1,0:T(8,128)(2,1)}), bf16[4,256,768]{2,1,0:T(8,128)(2,1)}, u32[]{:S(2)}, u32[]{:S(2)}) async-start(bf16[4,256,768]{2,1,0:T(8,128)(2,1)} %bitcast.266), calls=%async_computation.2 | async-start | bytes 3145728 | tf_op jit(solution)/shard_map/all_to_all | solution.py:185
  108.2 4.6 copy-start.56
  123.5 31.3 %all-to-all-start.1 = ((bf16[4,256,768]{2,1,0:T(8,128)(2,1)}), bf16[4,256,768]{2,1,0:T(8,128)(2,1)}, u32[]{:S(2)}, u32[]{:S(2)}) async-start(bf16[4,256,768]{2,1,0:T(8,128)(2,1)} %fusion.40), calls=%async_computation.1 | async-start | bytes 3145728 | tf_op jit(solution)/shard_map/all_to_all | solution.py:148
  143.6 2.7 copy-start.55
  154.8 26.3 %all-to-all-start.3 = ((bf16[4,256,768]{2,1,0:T(8,128)(2,1)}), bf16[4,256,768]{2,1,0:T(8,128)(2,1)}, u32[]{:S(2)}, u32[]{:S(2)}) async-start(bf16[4,256,768]{2,1,0:T(8,128)(2,1)} %fusion.45), calls=%async_computation.3 | async-start | bytes 3145728 | tf_op jit(solution)/shard_map/all_to_all | solution.py:206
  159.2 135.2 %reduce-scatter.18.cloned.1.call-start = ((), (), s32[]{:S(2)}) async-start(), calls=%async_computation.16 | async-start | bytes 1327104 | tf_op jit(solution)/shard_map/reduce_scatter | solution.py:295
  189.6 7.2 copy-start.35
  196.8 3.6 copy-start.6
  196.8 3.6 copy-start.17
  196.8 3.6 copy-start.18
  196.8 3.6 copy-start.22
  196.8 3.6 copy-start.42
  196.8 3.6 copy-start.44
  196.8 3.6 copy-start.51
  200.4 7.7 copy-start.16
  207.2 0.9 copy-start.9
  209.6 148.9 %reduce-scatter.16.cloned.1.call-start = ((), (), s32[]{:S(2)}) async-start(), calls=%async_computation.15 | async-start | bytes 3981312 | tf_op jit(solution)/shard_map/reduce_scatter | solution.py:292
  215.3 3.2 copy-start.2
  218.5 1.3 copy-start.8
  219.8 1.0 copy-start.13
  220.8 1.9 copy-start.4
  220.8 1.9 copy-start.24
  220.8 1.9 copy-start.29
  220.8 1.9 copy-start.34
  220.8 1.9 copy-start.40
  221.6 1.0 copy-start.12
  225.8 231.4 %reduce-scatter.20.cloned.1.call-start = ((), (), s32[]{:S(2)}) async-start(), calls=%async_computation.17 | async-start | bytes 5308416 | tf_op jit(solution)/shard_map/reduce_scatter | solution.py:298
  231.1 324.8 %reduce-scatter.22.cloned.1.call-start = ((), (), s32[]{:S(2)}) async-start(), calls=%async_computation.18 | async-start | bytes 5308416 | tf_op jit(solution)/shard_map/reduce_scatter | solution.py:301
  238.2 1.6 copy-start.25
  238.2 450.0 %reduce-scatter.14.cloned.1.call-start = ((), (), s32[]{:S(2)}) async-start(), calls=%async_computation.14 | async-start | bytes 7962624 | tf_op jit(solution)/shard_map/reduce_scatter | solution.py:286
  254.9 497.6 %reduce-scatter.28.cloned.1.call-start = ((), (), s32[]{:S(2)}) async-start(), calls=%async_computation.21 | async-start | bytes 221184
  258.1 5.6 copy-start.53
  263.6 549.7 %reduce-scatter.12.cloned.1.call-start = ((), (), s32[]{:S(2)}) async-start(), calls=%async_computation.13 | async-start | bytes 110592 | tf_op jit(solution)/shard_map/reduce_scatter | solution.py:283
  264.4 647.4 %reduce-scatter.26.cloned.1.call-start = ((), (), s32[]{:S(2)}) async-start(), calls=%async_computation.20 | async-start | bytes 5308416 | tf_op jit(solution)/shard_map/reduce_scatter | solution.py:310
  276.6 734.9 %reduce-scatter.24.cloned.1.call-start = ((), (), s32[]{:S(2)}) async-start(), calls=%async_computation.19 | async-start | bytes 5308416 | tf_op jit(solution)/shard_map/reduce_scatter | solution.py:307
  285.7 2.0 copy-start.37
  285.7 5.1 copy-start.36
  285.7 5.7 copy-start.38
  285.8 789.4 %all-reduce.5.cloned.1.call-start = ((), (), s32[]{:S(2)}) async-start(), calls=%async_computation.22 | async-start | bytes 5308416 | tf_op jit(solution)/shard_map/psum | solution.py:316
  1075.2 4.8 copy-start.19
  1075.2 5.9 copy-start.20
  1075.2 6.9 copy-start.27
  (7 other events, 5.2 us)
Sparse Core Ops, SparseCore 0:
  209.7 67.1 reduce-scatter.17
  280.5 77.9 reduce-scatter.15
  362.2 94.9 reduce-scatter.19
  460.7 95.1 reduce-scatter.21
  559.4 128.7 reduce-scatter.13
  692.3 60.1 reduce-scatter.27
  756.7 56.5 reduce-scatter.11
  817.4 94.4 reduce-scatter.25
  915.9 95.5 reduce-scatter.23
  1014.2 60.9 all-reduce.4
where the time goes:
time: 1100 us; the launch traced here: 1090 us
  waiting for transfers between devices  720 us (65%)
  matrix products  138 us (13%)
  local copies, waits for them, and re-layouts  79.9 us (7%)
  other arithmetic  69.3 us (6%)
  blocking collectives  46.5 us (4%)
  starting transfers between devices  19 us (2%)
  between operations  17.2 us (2%)
    reduce_scatter x1, waiting for transfers between devices, per_device(): lax.psum_scatter(grad_ada_weight.astype(jnp.bfloat16), 'grp', scatter_dim...  132 us
    reduce_scatter x1, waiting for transfers between devices, per_device(): lax.psum_scatter(grad_shared_down.astype(jnp.bfloat16), 'grp', scatter_di...  98.7 us
    reduce_scatter x1, waiting for transfers between devices, per_device(): lax.psum_scatter(grad_shared_up.astype(jnp.bfloat16), 'grp', scatter_dime...  98.6 us
    reduce_scatter x1, waiting for transfers between devices, per_device(): lax.psum_scatter(expert_up_grad.astype(jnp.bfloat16), 'grp', scatter_dime...  97.5 us
    reduce_scatter x1, waiting for transfers between devices, per_device(): lax.psum_scatter(expert_down_grad.astype(jnp.bfloat16), 'grp', scatter_di...  84.2 us
    reduce_scatter x1, waiting for transfers between devices, per_device(): lax.psum_scatter(grad_qkv.astype(jnp.bfloat16), 'grp', scatter_dimension=...  64.1 us
    psum x1, waiting for transfers between devices, per_device(): lax.psum(shares[1].astype(jnp.bfloat16), 'dp').astype(jnp.float32)  61.5 us
    reduce_scatter x1, waiting for transfers between devices, per_device(): lax.psum_scatter(grad_table.astype(jnp.bfloat16), 'grp', scatter_dimensio...  59.4 us
  transfers between devices with their start and end apart: 14, of which 9 were waited for; matrix products, arithmetic and copies ran while one was open for 17% of the time, Pallas kernels for 0%

commit v1 on v0

v1 whole, which is shorter than its diff:
```python
import jax
import jax.numpy as jnp
from jax import lax
from jax.sharding import PartitionSpec as P

HEADS = 12
TOP = 2


EPSILON = 1e-06


def product(left_mat, right_mat):
    return jnp.dot(left_mat, right_mat, preferred_element_type=jnp.float32)


def product_tn(left_mat, right_mat):
    return lax.dot_general(
        left_mat, right_mat, (((0,), (0,)), ((), ())), preferred_element_type=jnp.float32
    )


def product_nt(left_mat, right_mat):
    return lax.dot_general(
        left_mat, right_mat, (((1,), (1,)), ((), ())), preferred_element_type=jnp.float32
    )


def to_low(tensor):
    return tensor.astype(jnp.bfloat16)


def wide(tensor):
    return tensor.astype(jnp.float32)


def normalize(tensor):
    average = jnp.mean(tensor, axis=-1, keepdims=True)
    centered = tensor - average
    inverse = lax.rsqrt(jnp.mean(centered * centered, axis=-1, keepdims=True) + EPSILON)
    return (centered * inverse, inverse)


def normalize_back(gradient, normed, inverse):
    first_term = jnp.mean(gradient, axis=-1, keepdims=True)
    second_term = jnp.mean(gradient * normed, axis=-1, keepdims=True)
    return inverse * (gradient - first_term - normed * second_term)


def local_back(function, tensor, gradient):
    return jax.vjp(function, tensor)[1](gradient)[0]


def swap(tensor, axis, bit):
    pairs = [(i, i ^ (1 << bit)) for i in range(lax.axis_size(axis))]
    return lax.ppermute(tensor, axis, pairs)


def bits_of(axis):
    return lax.axis_size(axis).bit_length() - 1


def halve(tensor, place, axis, bit):
    mine = (lax.axis_index(axis) >> bit) & 1
    send = lax.dynamic_index_in_dim(tensor, 1 - mine, place, keepdims=False)
    keep = lax.dynamic_index_in_dim(tensor, mine, place, keepdims=False)
    return to_low(wide(keep) + wide(swap(send, axis, bit)))


def scatter_sum(tensor, axis, order):
    count = bits_of(axis)
    tensor = tensor.reshape((2,) * count + tensor.shape[1:])
    left = list(range(count - 1, -1, -1))
    for bit in order:
        place = left.index(bit)
        left.remove(bit)
        tensor = halve(tensor, place, axis, bit)
    return tensor


def gather_near(tensor, axis):
    blocks = {0: tensor}
    for bit in range(bits_of(axis) - 1, -1, -1):
        for far in list(blocks):
            blocks[far ^ (1 << bit)] = swap(blocks[far], axis, bit)
    return [blocks[i] for i in range(len(blocks))]


def gather_order(tensor, axis):
    me = lax.axis_index(axis)
    blocks = jnp.stack(gather_near(tensor, axis))
    return jnp.stack(
        [lax.dynamic_index_in_dim(blocks, i ^ me, 0, keepdims=False) for i in range(blocks.shape[0])]
    )


def return_near(blocks, axis):
    blocks = dict(enumerate(blocks))
    for bit in range(bits_of(axis)):
        for far in [r for r in blocks if r >> bit & 1]:
            got = swap(to_low(blocks.pop(far)), axis, bit)
            blocks[far ^ (1 << bit)] = wide(blocks[far ^ (1 << bit)]) + wide(got)
    return blocks[0]


def per_device(
    tokens,
    condition,
    bucket,
    live_mask,
    routes,
    bucket_table,
    ada_weight,
    ada_bias,
    qkv_weight,
    proj_weight,
    shared_up,
    shared_down,
    router_weight,
    expert_up,
    expert_down,
    cotangent,
):
    image_count, patch_count, width = tokens.shape
    rows = image_count * patch_count
    head = width // HEADS
    scaling = float(head) ** (-0.5)
    members, groups = lax.axis_size("dp"), lax.axis_size("grp")
    me, group = lax.axis_index("dp"), lax.axis_index("grp")
    experts = expert_up.shape[0] * members
    hidden = shared_up.shape[1]
    table_rows = bucket_table.shape[0]
    own_up, own_down = expert_up[0], expert_down[0]

    inputs = wide(tokens[0])
    selector = wide(bucket[:, None] == jnp.arange(table_rows, dtype=jnp.int32)[None, :])
    conditioned = wide(condition) + jnp.dot(
        selector, wide(bucket_table), precision=lax.Precision.HIGHEST
    )
    activated = to_low(jax.nn.silu(conditioned))
    modulation = product(activated, ada_weight) + wide(ada_bias)
    shift_attn, scale_attn, gate_attn, shift_mix, scale_mix, gate_mix = jnp.split(
        modulation, 6, axis=1
    )
    alive = wide(live_mask)[0]
    grad_result = wide(cotangent[0]) * alive
    grad_mixture = to_low(gate_mix * grad_result)
    expert_ids = jnp.arange(experts, dtype=jnp.int32)
    chosen = jnp.any(routes[0][:, :, None] == expert_ids[None, None, :], axis=1)
    grads_in = jnp.concatenate(
        [grad_mixture, jnp.pad(to_low(chosen), ((0, 0), (0, 128 - experts)))], axis=1
    )
    grads_in = jnp.concatenate(gather_near(grads_in, "dp"), axis=0)

    normed_one, inverse_one = normalize(inputs)
    attn_in = to_low(normed_one * (1.0 + scale_attn) + shift_attn)
    projected = to_low(product(attn_in, qkv_weight)).reshape(rows, 3, HEADS, head)
    query, key, value = [projected[:, i] for i in range(3)]
    scores = jnp.einsum("qhd,khd->hqk", query, key, preferred_element_type=jnp.float32) * scaling
    top_score = jnp.max(scores, axis=-1, keepdims=True)
    weights_exp = jnp.exp(scores - top_score)
    totals = jnp.sum(weights_exp, axis=-1, keepdims=True)
    log_total = top_score + jnp.log(totals)
    probs_first = to_low(weights_exp / totals)
    attended = jnp.einsum("hqk,khd->qhd", probs_first, value, preferred_element_type=jnp.float32)
    attended = to_low(attended.reshape(rows, width))
    attn_out = product(attended, proj_weight)
    middle = inputs + gate_attn * attn_out
    normed_two, inverse_two = normalize(middle)
    mix_in = to_low(normed_two * (1.0 + scale_mix) + shift_mix)

    seen = jnp.concatenate(gather_near(mix_in, "dp"), axis=0)
    grad_seen, seen_hot = grads_in[:, :width], wide(grads_in[:, width : width + experts])
    logits = product(seen, router_weight)
    top_logit = jnp.max(jnp.where(seen_hot > 0, logits, -jnp.inf), axis=1, keepdims=True)
    gates = jnp.where(seen_hot > 0, jnp.exp(logits - top_logit), 0.0)
    gates = gates / jnp.sum(gates, axis=1, keepdims=True)
    mine_hot = wide(expert_ids == me)[None, :]
    gate = jnp.sum(gates * mine_hot, axis=1, keepdims=True)

    part = hidden // (groups * members)
    part_up = lax.dynamic_index_in_dim(
        shared_up.reshape(width, groups, members, part), me, 2, keepdims=False
    ).reshape(width, groups * part)
    part_down = lax.dynamic_index_in_dim(
        shared_down.reshape(groups, members, part, width), me, 1, keepdims=False
    ).reshape(groups * part, width)

    def feed(up, down, grads):
        pre = product(seen, up)
        act = to_low(jax.nn.gelu(pre))
        out = product(act, down)
        grad_down = to_low(product_tn(act, grads))
        grad_pre = to_low(local_back(jax.nn.gelu, pre, product_nt(grads, down)))
        grad_up = to_low(product_tn(seen, grad_pre))
        return out, product_nt(grad_pre, up), grad_up, grad_down

    shared_out, shared_back, grad_part_up, grad_part_down = feed(part_up, part_down, grad_seen)
    grad_routed = to_low(gate * wide(grad_seen))
    routed, routed_back, grad_own_up, grad_own_down = feed(own_up, own_down, grad_routed)
    routed = wide(to_low(routed))
    weighed = jnp.sum(wide(grad_routed) * routed, axis=1, keepdims=True) * mine_hot
    weighed_high = to_low(weighed)
    weighed_low = to_low(weighed - wide(weighed_high))
    back = jnp.concatenate(
        [
            to_low(shared_back + routed_back),
            weighed_high,
            weighed_low,
            jnp.zeros((members * rows, 128 - 2 * experts), jnp.bfloat16),
        ],
        axis=1,
    )
    mixed = to_low(shared_out + gate * routed)
    back = return_near(jnp.split(back, members), "dp")
    mixture = return_near(jnp.split(mixed, members), "dp")

    result = (middle + gate_mix * mixture) * alive
    mixed_out = to_low(result)
    grad_gate_mix = jnp.sum(grad_result * mixture, axis=0, keepdims=True)
    weighed = back[:, width : width + experts] + back[:, width + experts : width + 2 * experts]
    own_gates = gates[:rows]
    grad_logits = to_low(weighed - own_gates * jnp.sum(weighed, axis=1, keepdims=True))
    grad_router = product_tn(mix_in, grad_logits)
    grad_mix_in = back[:, :width] + product_nt(grad_logits, router_weight)
    grad_shift_mix = jnp.sum(grad_mix_in, axis=0, keepdims=True)
    grad_scale_mix = jnp.sum(grad_mix_in * normed_two, axis=0, keepdims=True)
    grad_middle = grad_result + normalize_back(
        grad_mix_in * (1.0 + scale_mix), normed_two, inverse_two
    )
    grad_gate_attn = jnp.sum(grad_middle * attn_out, axis=0, keepdims=True)
    grad_attn_out = to_low(gate_attn * grad_middle)
    grad_proj = product_tn(attended, grad_attn_out)
    grad_attended = to_low(product_nt(grad_attn_out, proj_weight)).reshape(rows, HEADS, head)
    scores_again = (
        jnp.einsum("qhd,khd->hqk", query, key, preferred_element_type=jnp.float32) * scaling
    )
    probs_again = jnp.exp(scores_again - log_total)
    grad_probs = jnp.einsum(
        "qhd,khd->hqk", grad_attended, value, preferred_element_type=jnp.float32
    )
    grad_value = jnp.einsum(
        "hqk,qhd->khd", to_low(probs_again), grad_attended, preferred_element_type=jnp.float32
    )
    grad_scores = to_low(
        probs_again * (grad_probs - jnp.sum(probs_again * grad_probs, axis=-1, keepdims=True))
    )
    grad_query = (
        jnp.einsum("hqk,khd->qhd", grad_scores, key, preferred_element_type=jnp.float32) * scaling
    )
    grad_key = (
        jnp.einsum("hqk,qhd->khd", grad_scores, query, preferred_element_type=jnp.float32) * scaling
    )
    grad_projected = to_low(
        jnp.stack([grad_query, grad_key, grad_value], axis=1).reshape(rows, 3 * width)
    )
    grad_qkv = product_tn(attn_in, grad_projected)
    grad_attn_in = product_nt(grad_projected, qkv_weight)
    grad_shift_attn = jnp.sum(grad_attn_in, axis=0, keepdims=True)
    grad_scale_attn = jnp.sum(grad_attn_in * normed_one, axis=0, keepdims=True)
    grad_tokens = grad_middle + normalize_back(
        grad_attn_in * (1.0 + scale_attn), normed_one, inverse_one
    )
    grad_modulation = jnp.concatenate(
        [
            grad_shift_attn,
            grad_scale_attn,
            grad_gate_attn,
            grad_shift_mix,
            grad_scale_mix,
            grad_gate_mix,
        ],
        axis=1,
    )
    grad_mod_low = to_low(grad_modulation)
    grad_condition = local_back(jax.nn.silu, conditioned, product_nt(grad_mod_low, ada_weight))

    share = table_rows // groups
    near = wide(bucket[:, None] == group * share + jnp.arange(share, dtype=jnp.int32)[None, :])
    table_part = near.T * grad_condition
    for bit in range(bits_of("dp")):
        table_part = table_part + swap(table_part, "dp", bit)

    factors = jnp.concatenate([activated, grad_mod_low], axis=1)
    for axis in ("dp", "grp"):
        for bit in range(bits_of(axis)):
            factors = jnp.concatenate([factors, swap(factors, axis, bit)], axis=0)
    shard = width // groups
    left = lax.dynamic_slice_in_dim(factors[:, :width], group * shard, shard, axis=1)
    right = factors[:, width:]
    ada_w_part = product_tn(left, right)
    ada_share = 6 * width // groups
    ada_b_part = jnp.sum(
        wide(lax.dynamic_slice_in_dim(right, group * ada_share, ada_share, axis=1)), axis=0
    )

    y_first = tuple(range(bits_of("grp")))
    z_first = y_first[1:] + y_first[:1]

    def over_groups(tensor, order):
        return scatter_sum(
            tensor.reshape((groups, tensor.shape[0] // groups) + tensor.shape[1:]), "grp", order
        )

    up_part = over_groups(grad_part_up, z_first)
    down_part = over_groups(grad_part_down, y_first)
    expert_up_part = over_groups(grad_own_up, y_first)
    expert_down_part = over_groups(grad_own_down, y_first)
    up_part = wide(gather_order(up_part, "dp")).reshape(members, shard, groups, part)
    up_part = up_part.transpose(1, 2, 0, 3).reshape(shard, hidden)
    down_part = wide(gather_order(down_part, "dp")).reshape(hidden // groups, width)

    def over_all(tensor):
        tensor = to_low(tensor)
        columns = tensor.shape[1]
        tensor = tensor.reshape(groups, members, -1, columns).swapaxes(0, 1)
        tensor = scatter_sum(tensor, "dp", range(bits_of("dp")))
        tensor = scatter_sum(tensor, "grp", y_first)
        return wide(gather_order(tensor, "dp")).reshape(-1, columns)

    proj_part = over_all(
        jnp.concatenate(
            [grad_proj, grad_router, jnp.zeros((width, 128 - experts), jnp.float32)], axis=1
        )
    )
    qkv_part = over_all(grad_qkv)
    return (
        mixed_out[None],
        grad_tokens[None],
        grad_condition,
        table_part,
        ada_w_part,
        ada_b_part,
        qkv_part,
        proj_part[:, :width],
        up_part,
        down_part,
        proj_part[:, width : width + experts],
        wide(expert_up_part)[None],
        wide(expert_down_part)[None],
    )


def solution(mesh):
    in_specs = (
        P(("grp", "dp"), None, None),
        P(("grp", "dp"), None),
        P(("grp", "dp")),
        P(("grp", "dp")),
        P(("grp", "dp"), None, None),
        P(),
        P(),
        P(),
        P(),
        P(),
        P(),
        P(),
        P(),
        P("dp", None, None),
        P("dp", None, None),
        P(("grp", "dp"), None, None),
    )
    out_specs = (
        P(("grp", "dp"), None, None),
        P(("grp", "dp"), None, None),
        P(("grp", "dp"), None),
        P("grp", None),
        P("grp", None),
        P("grp"),
        P("grp", None),
        P("grp", None),
        P("grp", None),
        P("grp", None),
        P("grp", None),
        P("dp", "grp", None),
        P("dp", "grp", None),
    )
    return jax.shard_map(
        per_device, mesh=mesh, in_specs=in_specs, out_specs=out_specs, check_vma=False
    )
```

time: 1100 us -> 524 us (0.48)
  waiting for transfers between devices: 720 us -> 194 us
  blocking collectives: 46.5 us -> 0 us
  local copies, waits for them, and re-layouts: 79.9 us -> 98 us
  starting transfers between devices: 19 us -> 33.7 us
  other arithmetic: 69.3 us -> 55.1 us
  between operations: 17.2 us -> 4.02 us
    reduce_scatter x8 -> x0, waiting for transfers between devices: 635 us -> none  [the longest x1 132 us: per_device(): lax.psum_scatter(grad_ada_weight.astype(jnp.bfloat16), 'grp', scatter_dim...]
    ppermute x0 -> x53, waiting for transfers between devices: none -> 194 us  [swap(): return lax.ppermute(tensor, axis, pairs)]
    dot_general x13 -> x7, matrix products: 73.5 us -> 11.4 us  [the longest x1 2.82 us: per_device(): jnp.einsum('hqk,qhd->khd', to_low(probs_again), grad_attended, preferred_...]
    psum x1 -> x0, waiting for transfers between devices: 61.5 us -> none  [per_device(): lax.psum(shares[1].astype(jnp.bfloat16), 'dp').astype(jnp.float32)]
    unnamed x1 -> x0, blocking collectives: 35.3 us -> none
    ppermute x0 -> x53, starting transfers between devices: none -> 33.7 us  [swap(): return lax.ppermute(tensor, axis, pairs)]
    unnamed x11 -> x0, waiting for transfers between devices: 23.6 us -> none
    convert_element_type x2 -> x27, other arithmetic: 0.9 us -> 23.4 us  [to_low(): return tensor.astype(jnp.bfloat16)]
  transfers between devices with their start and end apart: 14 -> 53, of which waited for: 9 -> 20; matrix products, arithmetic and copies ran while one was open for 17% -> 47% of each run, Pallas kernels for 0% -> 0%
where the time goes in v1:
time: 524 us; the launch traced here: 515 us
  waiting for transfers between devices  194 us (37%)
  matrix products  130 us (25%)
  local copies, waits for them, and re-layouts  98 us (19%)
  other arithmetic  55.1 us (11%)
  starting transfers between devices  33.7 us (6%)
    ppermute x53, waiting for transfers between devices, swap(): return lax.ppermute(tensor, axis, pairs)  194 us
    dot_general x8, matrix products, product_nt(): lax.dot_general(left_mat, right_mat, (((1,), (1,)), ((), ())), preferred_...  45.8 us
    unnamed x186, local copies, waits for them, and re-layouts  41 us
    dot_general x8, matrix products, product(): return jnp.dot(left_mat, right_mat, preferred_element_type=jnp.float32)  38.4 us
    dot_general x8, matrix products, product_tn(): lax.dot_general(left_mat, right_mat, (((0,), (0,)), ((), ())), preferred_...  34.2 us
    ppermute x53, starting transfers between devices, swap(): return lax.ppermute(tensor, axis, pairs)  33.7 us
    convert_element_type x27, other arithmetic, to_low(): return tensor.astype(jnp.bfloat16)  23.4 us
  transfers between devices with their start and end apart: 53, of which 20 were waited for; matrix products, arithmetic and copies ran while one was open for 47% of the time, Pallas kernels for 0%

profile of v1, /device:TPU:0, one launch (start us, length us, event | category | flops | bytes accessed | tf_op | source)
XLA Modules:
  0.0 514.6 jit_solution(13119106498940704279)
XLA Ops:
  3.3 4.1 convolution_reduce_fusion
  8.0 2.0 copy.119
  12.8 3.3 convolution_convert_fusion.3
  16.1 2.4 copy.120
  20.8 2.2 fusion.47
  26.5 2.9 collective-permute-start.1
  30.1 1.9 copy.124
  35.9 2.4 constant_dynamic-slice_fusion.23
  41.5 6.6 %copy.123 = bf16[768,3072]{0,1:T(8,128)(2,1)} copy(bf16[768,3072]{1,0:T(8,128)(2,1)} %param.26) | data formatting | bytes 9437184 | tf_op args[10]
  50.9 8.0 %fusion.15 = f32[1024,3072]{1,0:T(8,128)S(1)} fusion(bf16[1,768,3072]{2,1,0:T(8,128)(2,1)} %param.29, bf16[256,768]{0,1:T(8,128)(2,1)} %collective-permute-done.2, bf16[256,768]{0,1:T(8,128)(2,1)} %collective-permute-done.1, bf16[256,768]{0,1:T(8,128)(2,1)} %collective-permute-done, bf16[256,768]{0,1:T(8,128)(2,1)} %add_convert_fusion.3), kind=kOutput, calls=%fused_computation.23 | convolution fusion | flops 4838129664 | bytes 18874368 | tf_op jit(solution)/shard_map/dot_general | solution.py:14
  59.0 4.1 fusion.129
  63.2 4.2 convolution_convert_fusion.4
  69.3 2.1 collective-permute-start.41
  71.4 4.2 fusion.27
  75.6 3.3 convolution_convert_fusion.5
  83.9 11.3 %fusion.20 = (f32[1024]{0:T(1024)S(1)}, bf16[1024,768]{0,1:T(8,128)(2,1)}) fusion(f32[1024]{0:T(1024)} %get-tuple-element.96, bf16[256,896]{0,1:T(8,128)(2,1)} %copy-done.76, bf16[256,896]{0,1:T(8,128)(2,1)} %collective-permute-done.4, bf16[256,896]{0,1:T(8,128)(2,1)} %collective-permute-done.3, bf16[256,128]{0,1:T(8,128)(2,1)S(1)} %copy-done.42, ...), kind=kOutput, calls=%fused_computation.34 | convolution fusion | flops 4873518080 | bytes 20717568 | tf_op jit(solution)/shard_map/dot_general | solution.py:14
  95.2 4.5 fusion.19
  101.7 21.3 %fusion.6 = bf16[1024,3072]{1,0:T(8,128)(2,1)} fusion(f32[1024,3072]{1,0:T(8,128)} %copy-done.9, bf16[1,3072,768]{2,1,0:T(8,128)(2,1)} %param.30, f32[1024]{0:T(1024)S(1)} %copy-done.72, bf16[256,896]{0,1:T(8,128)(2,1)S(1)} %copy-done.77, bf16[256,896]{0,1:T(8,128)(2,1)} %collective-permute-done.4, bf16[256,896]{0,1:T(8,128)(2,1)} %collective-permute-done.3, ...), kind=kOutput, calls=%fused_computation.8 | convolution fusion | flops 4904189952 | bytes 25432064 | tf_op jit(solution)/shard_map/dot_general | solution.py:24
  123.0 7.7 %fusion.13 = f32[1024,768]{0,1:T(8,128)S(1)} fusion(bf16[1024,3072]{1,0:T(8,128)(2,1)} %fusion.6, bf16[1,768,3072]{2,1,0:T(8,128)(2,1)S(1)} %bitcast.344), kind=kOutput, calls=%fused_computation.21 | convolution fusion | flops 4831838208 | bytes 14155776 | tf_op jit(solution)/shard_map/dot_general | solution.py:24
  132.8 2.6 copy-done.10
  135.3 9.5 %convolution_convert_fusion = bf16[3072,768]{1,0:T(8,128)(2,1)S(1)} fusion(f32[1024]{0:T(1024)S(1)} %copy-done.72, f32[1024,3072]{1,0:T(8,128)S(1)} %copy-done.10, bf16[256,896]{0,1:T(8,128)(2,1)} %copy-done.76, bf16[256,896]{0,1:T(8,128)(2,1)} %collective-permute-done.4, bf16[256,896]{0,1:T(8,128)(2,1)} %collective-permute-done.3, ...), kind=kOutput, calls=%fused_computation.10 | convolution fusion | flops 4871946240 | bytes 19140608 | tf_op jit(solution)/shard_map/dot_general | solution.py:18
  144.9 7.7 %convolution_convert_fusion.1 = bf16[768,3072]{1,0:T(8,128)(2,1)S(1)} fusion(bf16[1024,3072]{1,0:T(8,128)(2,1)} %fusion.6, bf16[256,768]{0,1:T(8,128)(2,1)} %collective-permute-done.2, bf16[256,768]{0,1:T(8,128)(2,1)} %collective-permute-done.1, bf16[256,768]{0,1:T(8,128)(2,1)} %collective-permute-done, bf16[256,768]{0,1:T(8,128)(2,1)} %add_convert_fusion.3), kind=kOutput, calls=%fused_computation.11 | convolution fusion | flops 4840488960 | bytes 12582912 | tf_op jit(solution)/shard_map/dot_general | solution.py:18
  167.0 7.4 %collective-permute-done.42 = bf16[2,96,768]{2,1,0:T(8,128)(2,1)S(1)} collective-permute-done((bf16[2,96,768]{2,1,0:T(8,128)(2,1)S(1)}, bf16[2,96,768]{2,1,0:T(8,128)(2,1)S(1)}, u32[]{:S(2)}, u32[]{:S(2)}) %collective-permute-start.42) | collective-permute-done | bytes 294944 | tf_op jit(solution)/shard_map/ppermute | solution.py:56
  174.5 2.6 collective-permute-start.36
  177.9 12.1 %collective-permute-done.36 = bf16[2,96,768]{2,1,0:T(8,128)(2,1)S(1)} collective-permute-done((bf16[2,96,768]{2,1,0:T(8,128)(2,1)S(1)}, bf16[2,96,768]{2,1,0:T(8,128)(2,1)S(1)}, u32[]{:S(2)}, u32[]{:S(2)}) %collective-permute-start.36) | collective-permute-done | bytes 294944 | tf_op jit(solution)/shard_map/ppermute | solution.py:56
  194.5 1.9 convolution_convert_fusion.8
  196.4 4.6 collective-permute-done.8
  201.0 3.1 fusion.75
  206.4 1.9 copy.128
  208.3 2.8 fusion.42
  211.3 1.9 multiply_reduce_fusion
  215.7 2.6 fusion.140
  218.3 3.0 convolution_convert_fusion.2
  221.3 1.9 copy.146
  224.8 1.8 convolution_convert_fusion.6
  229.8 2.3 copy.132
  232.0 2.4 fusion.68
  251.8 5.7 %fusion.133 = (f32[768]{0:T(1024)S(1)}, f32[1,768]{1,0:T(1,128)}) fusion(f32[1,768]{1,0:T(1,128)} %copy-done.64, bf16[4608,1]{0,1:T(2,128)(2,1)S(1)} %reshape.430, bf16[768,4608]{1,0:T(8,128)(2,1)} %param.22), kind=kOutput, calls=%fused_computation.312 | convolution fusion | flops 7084800 | bytes 7096320 | tf_op jit(solution)/shard_map/dot_general | solution.py:24
  263.2 2.3 copy.147
  268.2 2.5 collective-permute-done.15
  272.0 2.5 collective-permute-done.13
  282.3 2.3 collective-permute-done.17
  284.7 3.1 concatenate.84
  293.7 5.2 %collective-permute-done.18 = bf16[16,5376]{1,0:T(8,128)(2,1)} collective-permute-done((bf16[16,5376]{1,0:T(8,128)(2,1)}, bf16[16,5376]{1,0:T(8,128)(2,1)}, u32[]{:S(2)}, u32[]{:S(2)}) %collective-permute-start.18) | collective-permute-done | bytes 172064 | tf_op jit(solution)/shard_map/ppermute | solution.py:56
  300.0 4.7 concatenate.85
  307.2 2.7 fusion.108
  316.0 53.2 %collective-permute-done.29 = bf16[2,2,24,896]{3,2,1,0:T(8,128)(2,1)S(1)} collective-permute-done((bf16[2,2,24,896]{3,2,1,0:T(8,128)(2,1)S(1)}, bf16[2,2,24,896]{3,2,1,0:T(8,128)(2,1)S(1)}, u32[]{:S(2)}, u32[]{:S(2)}) %collective-permute-start.29) | collective-permute-done | bytes 172064 | tf_op jit(solution)/shard_map/ppermute | solution.py:56
  370.2 3.6 collective-permute-done.30
  374.1 4.8 collective-permute-done.31
  381.5 1.8 stack.130
  383.4 1.8 stack.131
  390.9 2.2 copy.141
  393.1 3.8 reshape.412
  400.8 3.1 fusion.7
  404.2 1.9 fusion.17
  407.7 2.6 fusion.8
  410.3 17.5 %collective-permute-done.20 = bf16[8,24,2304]{2,1,0:T(8,128)(2,1)S(1)} collective-permute-done((bf16[8,24,2304]{2,1,0:T(8,128)(2,1)S(1)}, bf16[8,24,2304]{2,1,0:T(8,128)(2,1)S(1)}, u32[]{:S(2)}, u32[]{:S(2)}) %collective-permute-start.20) | collective-permute-done | bytes 884768 | tf_op jit(solution)/shard_map/ppermute | solution.py:56
  429.7 6.6 %collective-permute-done.51 = bf16[2,384,768]{2,1,0:T(8,128)(2,1)S(1)} collective-permute-done((bf16[2,384,768]{2,1,0:T(8,128)(2,1)S(1)}, bf16[2,384,768]{2,1,0:T(8,128)(2,1)S(1)}, u32[]{:S(2)}, u32[]{:S(2)}) %collective-permute-start.51) | collective-permute-done | bytes 1179680 | tf_op jit(solution)/shard_map/ppermute | solution.py:56
  436.7 2.6 collective-permute-done.21
  439.5 34.7 %collective-permute-done.48 = bf16[2,96,3072]{2,1,0:T(8,128)(2,1)S(1)} collective-permute-done((bf16[2,96,3072]{2,1,0:T(8,128)(2,1)S(1)}, bf16[2,96,3072]{2,1,0:T(8,128)(2,1)S(1)}, u32[]{:S(2)}, u32[]{:S(2)}) %collective-permute-start.48) | collective-permute-done | bytes 1179680 | tf_op jit(solution)/shard_map/ppermute | solution.py:56
  474.6 3.1 collective-permute-done.22
  478.2 2.7 collective-permute-start.49
  480.9 16.8 %collective-permute-done.23 = bf16[24,2304]{1,0:T(8,128)(2,1)S(1)} collective-permute-done((bf16[24,2304]{1,0:T(8,128)(2,1)S(1)}, bf16[24,2304]{1,0:T(8,128)(2,1)S(1)}, u32[]{:S(2)}, u32[]{:S(2)}) %collective-permute-start.23) | collective-permute-done | bytes 110624 | tf_op jit(solution)/shard_map/ppermute | solution.py:56
  499.0 11.2 %collective-permute-done.49 = bf16[96,3072]{1,0:T(8,128)(2,1)S(1)} collective-permute-done((bf16[96,3072]{1,0:T(8,128)(2,1)S(1)}, bf16[96,3072]{1,0:T(8,128)(2,1)S(1)}, u32[]{:S(2)}, u32[]{:S(2)}) %collective-permute-start.49) | collective-permute-done | bytes 589856 | tf_op jit(solution)/shard_map/ppermute | solution.py:56
  (393 shorter events, 135.2 us)
Async XLA Ops:
  8.0 24.0 %copy-start.54 = (f32[768]{0:T(1024)}, f32[768]{0:T(1024)S(1)}, u32[]{:S(2)}) copy-start(f32[768]{0:T(1024)S(1)} %get-tuple-element.85) | copy-start | bytes 9220
  26.5 13.2 %collective-permute-start.1 = (bf16[256,768]{0,1:T(8,128)(2,1)}, bf16[256,768]{0,1:T(8,128)(2,1)}, u32[]{:S(2)}, u32[]{:S(2)}) collective-permute-start(bf16[256,768]{0,1:T(8,128)(2,1)} %add_convert_fusion.3), channel_id=1, source_target_pairs={{0,2},{1,3},{2,0},{3,1},{4,6},{5,7},{6,4},{7,5},{8,10},{9,11},{10,... | collective-permute-start | bytes 1179656 | tf_op jit(solution)/shard_map/ppermute | solution.py:56
  34.8 15.6 %collective-permute-start.4 = (bf16[256,896]{0,1:T(8,128)(2,1)}, bf16[256,896]{0,1:T(8,128)(2,1)}, u32[]{:S(2)}, u32[]{:S(2)}) collective-permute-start(bf16[256,896]{0,1:T(8,128)(2,1)} %pad_maximum_fusion.8), channel_id=1, source_target_pairs={{0,2},{1,3},{2,0},{3,1},{4,6},{5,7},{6,4},{7,5},{8,10},{9,11},{10,... | collective-permute-start | bytes 1376264 | tf_op jit(solution)/shard_map/ppermute | solution.py:56
  34.8 28.4 %collective-permute-start.3 = (bf16[256,896]{0,1:T(8,128)(2,1)}, bf16[256,896]{0,1:T(8,128)(2,1)}, u32[]{:S(2)}, u32[]{:S(2)}) collective-permute-start(bf16[256,896]{0,1:T(8,128)(2,1)} %pad_maximum_fusion.8), channel_id=1, source_target_pairs={{0,1},{1,0},{2,3},{3,2},{4,5},{5,4},{6,7},{7,6},{8,9},{9,8},{10,11... | collective-permute-start | bytes 1376264 | tf_op jit(solution)/shard_map/ppermute | solution.py:56
  34.8 16.2 %collective-permute-start = (bf16[256,768]{0,1:T(8,128)(2,1)}, bf16[256,768]{0,1:T(8,128)(2,1)}, u32[]{:S(2)}, u32[]{:S(2)}) collective-permute-start(bf16[256,768]{0,1:T(8,128)(2,1)} %add_convert_fusion.3), channel_id=1, source_target_pairs={{0,1},{1,0},{2,3},{3,2},{4,5},{5,4},{6,7},{7,6},{8,9},{9,8},{10,11... | collective-permute-start | bytes 1179656 | tf_op jit(solution)/shard_map/ppermute | solution.py:56
  39.7 11.3 %collective-permute-start.2 = (bf16[256,768]{0,1:T(8,128)(2,1)}, bf16[256,768]{0,1:T(8,128)(2,1)}, u32[]{:S(2)}, u32[]{:S(2)}) collective-permute-start(bf16[256,768]{0,1:T(8,128)(2,1)} %collective-permute-done.1), channel_id=1, source_target_pairs={{0,1},{1,0},{2,3},{3,2},{4,5},{5,4},{6,7},{7,6},{8,9},{9,8},{10,11... | collective-permute-start | bytes 1179656 | tf_op jit(solution)/shard_map/ppermute | solution.py:56
  50.4 12.8 %collective-permute-start.5 = (bf16[256,896]{0,1:T(8,128)(2,1)}, bf16[256,896]{0,1:T(8,128)(2,1)S(1)}, u32[]{:S(2)}, u32[]{:S(2)}) collective-permute-start(bf16[256,896]{0,1:T(8,128)(2,1)} %collective-permute-done.4), channel_id=1, source_target_pairs={{0,1},{1,0},{2,3},{3,2},{4,5},{5,4},{6,7},{7,6},{8,9},{9,8},{10,11... | collective-permute-start | bytes 1376264 | tf_op jit(solution)/shard_map/ppermute | solution.py:56
  59.0 24.9 %copy-start.9 = (f32[1024,3072]{1,0:T(8,128)}, f32[1024,3072]{1,0:T(8,128)S(1)}, u32[]{:S(2)}) copy-start(f32[1024,3072]{1,0:T(8,128)S(1)} %fusion.15) | copy-start | bytes 37748740
  69.3 93.1 %collective-permute-start.41 = (bf16[2,2,96,768]{3,2,1,0:T(8,128)(2,1)}, bf16[2,2,96,768]{3,2,1,0:T(8,128)(2,1)}, u32[]{:S(2)}, u32[]{:S(2)}) collective-permute-start(bf16[2,2,96,768]{3,2,1,0:T(8,128)(2,1)} %dynamic-slice_bitcast_fusion.6), channel_id=1, source_target_pairs={{0,4},{4,0},{8,12},{12,8},{16,20},{20,16},{24,28},{28,24},{1,5},{5... | collective-permute-start | bytes 1769480 | tf_op jit(solution)/shard_map/ppermute | solution.py:56
  79.9 85.4 %collective-permute-start.35 = (bf16[2,2,96,768]{3,2,1,0:T(8,128)(2,1)}, bf16[2,2,96,768]{3,2,1,0:T(8,128)(2,1)}, u32[]{:S(2)}, u32[]{:S(2)}) collective-permute-start(bf16[2,2,96,768]{3,2,1,0:T(8,128)(2,1)} %dynamic-slice_bitcast_fusion.7), channel_id=1, source_target_pairs={{0,8},{4,12},{8,0},{12,4},{16,24},{20,28},{24,16},{28,20},{1,9},{5... | collective-permute-start | bytes 1769480 | tf_op jit(solution)/shard_map/ppermute | solution.py:56
  101.1 95.3 %collective-permute-start.6 = (bf16[256,768]{0,1:T(8,128)(2,1)}, bf16[256,768]{0,1:T(8,128)(2,1)}, u32[]{:S(2)}, u32[]{:S(2)}) collective-permute-start(bf16[256,768]{0,1:T(8,128)(2,1)} %get-tuple-element.110), channel_id=1, source_target_pairs={{0,1},{1,0},{2,3},{3,2},{4,5},{5,4},{6,7},{7,6},{8,9},{9,8},{10,11... | collective-permute-start | bytes 1179656 | tf_op jit(solution)/shard_map/ppermute | solution.py:56
  101.1 21.8 %slice-start.1 = ((s8[4718592]{0:T(1024)(128)(4,1)}), s8[524288]{0:T(1024)(128)(4,1)S(1)}, s32[]{:S(2)}) async-start(s8[4718592]{0:T(1024)(128)(4,1)} %bitcast.343), calls=%async_computation.1 | async-start | bytes 1048576
  101.1 58.3 %collective-permute-start.7 = (bf16[256,768]{0,1:T(8,128)(2,1)}, bf16[256,768]{0,1:T(8,128)(2,1)}, u32[]{:S(2)}, u32[]{:S(2)}) collective-permute-start(bf16[256,768]{0,1:T(8,128)(2,1)} %get-tuple-element.111), channel_id=1, source_target_pairs={{0,1},{1,0},{2,3},{3,2},{4,5},{5,4},{6,7},{7,6},{8,9},{9,8},{10,11... | collective-permute-start | bytes 1179656 | tf_op jit(solution)/shard_map/ppermute | solution.py:56
  132.7 28.4 %collective-permute-start.10 = (bf16[256,896]{0,1:T(8,128)(2,1)S(1)}, bf16[256,896]{0,1:T(8,128)(2,1)}, u32[]{:S(2)}, u32[]{:S(2)}) collective-permute-start(bf16[256,896]{0,1:T(8,128)(2,1)S(1)} %get-tuple-element.109), channel_id=1, source_target_pairs={{0,1},{1,0},{2,3},{3,2},{4,5},{5,4},{6,7},{7,6},{8,9},{9,8},{10,11... | collective-permute-start | bytes 1376264 | tf_op jit(solution)/shard_map/ppermute | solution.py:56
  159.4 241.3 %collective-permute-start.50 = (bf16[2,2,384,768]{3,2,0,1:T(8,128)(2,1)}, bf16[2,2,384,768]{3,2,0,1:T(8,128)(2,1)}, u32[]{:S(2)}, u32[]{:S(2)}) collective-permute-start(bf16[2,2,384,768]{3,2,0,1:T(8,128)(2,1)} %bitcast.324), channel_id=1, source_target_pairs={{0,4},{4,0},{8,12},{12,8},{16,20},{20,16},{24,28},{28,24},{1,5},{5... | collective-permute-start | bytes 7077896 | tf_op jit(solution)/shard_map/ppermute | solution.py:56
  161.1 30.2 %collective-permute-start.9 = (bf16[256,896]{0,1:T(8,128)(2,1)S(1)}, bf16[256,896]{0,1:T(8,128)(2,1)S(1)}, u32[]{:S(2)}, u32[]{:S(2)}) collective-permute-start(bf16[256,896]{0,1:T(8,128)(2,1)S(1)} %get-tuple-element.108), channel_id=1, source_target_pairs={{0,1},{1,0},{2,3},{3,2},{4,5},{5,4},{6,7},{7,6},{8,9},{9,8},{10,11... | collective-permute-start | bytes 1376264 | tf_op jit(solution)/shard_map/ppermute | solution.py:56
  162.4 29.0 %collective-permute-start.11 = (bf16[256,896]{0,1:T(8,128)(2,1)S(1)}, bf16[256,896]{0,1:T(8,128)(2,1)S(1)}, u32[]{:S(2)}, u32[]{:S(2)}) collective-permute-start(bf16[256,896]{0,1:T(8,128)(2,1)S(1)} %add_convert_fusion.1), channel_id=1, source_target_pairs={{0,2},{1,3},{2,0},{3,1},{4,6},{5,7},{6,4},{7,5},{8,10},{9,11},{10,... | collective-permute-start | bytes 1376264 | tf_op jit(solution)/shard_map/ppermute | solution.py:56
  165.2 27.9 %copy-start.12 = (f32[256,768]{0,1:T(8,128)S(1)}, f32[256,768]{0,1:T(8,128)}, u32[]{:S(2)}) copy-start(f32[256,768]{0,1:T(8,128)} %copy-done.11) | copy-start | bytes 2359300
  165.2 27.9 %copy-start.57 = (f32[768]{0:T(1024)S(1)}, f32[768]{0:T(1024)}, u32[]{:S(2)}) copy-start(f32[768]{0:T(1024)} %get-tuple-element.87) | copy-start | bytes 9220
  165.2 27.9 %copy-start.63 = (f32[256]{0:T(256)S(1)}, f32[256]{0:T(256)}, u32[]{:S(2)}) copy-start(f32[256]{0:T(256)} %copy-done.62) | copy-start | bytes 3076
  165.2 27.9 %copy-start.67 = (f32[256]{0:T(256)S(1)}, f32[256]{0:T(256)}, u32[]{:S(2)}) copy-start(f32[256]{0:T(256)} %copy-done.66) | copy-start | bytes 3076
  165.2 27.9 %copy-start.79 = (bf16[768,4]{0,1:T(4,128)(2,1)S(1)}, bf16[768,4]{0,1:T(4,128)(2,1)}, u32[]{:S(2)}) copy-start(bf16[768,4]{0,1:T(4,128)(2,1)} %param.28) | copy-start | bytes 18436
  165.3 9.2 %collective-permute-start.42 = (bf16[2,96,768]{2,1,0:T(8,128)(2,1)S(1)}, bf16[2,96,768]{2,1,0:T(8,128)(2,1)S(1)}, u32[]{:S(2)}, u32[]{:S(2)}) collective-permute-start(bf16[2,96,768]{2,1,0:T(8,128)(2,1)S(1)} %dynamic-slice_bitcast_fusion.10), channel_id=1, source_target_pairs={{0,8},{4,12},{8,0},{12,4},{16,24},{20,28},{24,16},{28,20},{1,9},{5... | collective-permute-start | bytes 884744 | tf_op jit(solution)/shard_map/ppermute | solution.py:56
  174.5 15.5 %collective-permute-start.36 = (bf16[2,96,768]{2,1,0:T(8,128)(2,1)S(1)}, bf16[2,96,768]{2,1,0:T(8,128)(2,1)S(1)}, u32[]{:S(2)}, u32[]{:S(2)}) collective-permute-start(bf16[2,96,768]{2,1,0:T(8,128)(2,1)S(1)} %dynamic-slice_bitcast_fusion.11), channel_id=1, source_target_pairs={{0,16},{4,20},{8,24},{12,28},{16,0},{20,4},{24,8},{28,12},{1,17},{... | collective-permute-start | bytes 884744 | tf_op jit(solution)/shard_map/ppermute | solution.py:56
  177.2 23.9 %copy-start.20 = (bf16[1,256,768]{1,2,0:T(8,128)(2,1)S(1)}, bf16[1,256,768]{1,2,0:T(8,128)(2,1)}, u32[]{:S(2)}) copy-start(bf16[1,256,768]{1,2,0:T(8,128)(2,1)} %copy.124) | copy-start | bytes 1179652
  177.2 23.8 %copy-start.22 = (f32[256,768]{0,1:T(8,128)S(1)}, f32[256,768]{0,1:T(8,128)}, u32[]{:S(2)}) copy-start(f32[256,768]{0,1:T(8,128)} %get-tuple-element.136) | copy-start | bytes 2359300
  177.2 23.8 %copy-start.55 = (f32[768]{0:T(1024)S(1)}, f32[768]{0:T(1024)}, u32[]{:S(2)}) copy-start(f32[768]{0:T(1024)} %copy-done.54) | copy-start | bytes 9220
  190.0 11.0 %collective-permute-start.8 = (bf16[256,768]{0,1:T(8,128)(2,1)S(1)}, bf16[256,768]{0,1:T(8,128)(2,1)S(1)}, u32[]{:S(2)}, u32[]{:S(2)}) collective-permute-start(bf16[256,768]{0,1:T(8,128)(2,1)S(1)} %add_convert_fusion.2), channel_id=1, source_target_pairs={{0,2},{1,3},{2,0},{3,1},{4,6},{5,7},{6,4},{7,5},{8,10},{9,11},{10,... | collective-permute-start | bytes 1179656 | tf_op jit(solution)/shard_map/ppermute | solution.py:56
  191.4 88.7 %collective-permute-start.43 = (bf16[96,768]{1,0:T(8,128)(2,1)}, bf16[96,768]{1,0:T(8,128)(2,1)}, u32[]{:S(2)}, u32[]{:S(2)}) collective-permute-start(bf16[96,768]{1,0:T(8,128)(2,1)} %dynamic-slice_bitcast_fusion.14), channel_id=1, source_target_pairs={{0,16},{4,20},{8,24},{12,28},{16,0},{20,4},{24,8},{28,12},{1,17},{... | collective-permute-start | bytes 442376 | tf_op jit(solution)/shard_map/ppermute | solution.py:56
  191.4 99.6 %collective-permute-start.37 = (bf16[96,768]{1,0:T(8,128)(2,1)}, bf16[96,768]{1,0:T(8,128)(2,1)}, u32[]{:S(2)}, u32[]{:S(2)}) collective-permute-start(bf16[96,768]{1,0:T(8,128)(2,1)} %dynamic-slice_bitcast_fusion.15), channel_id=1, source_target_pairs={{0,4},{4,0},{8,12},{12,8},{16,20},{20,16},{24,28},{28,24},{1,5},{5... | collective-permute-start | bytes 442376 | tf_op jit(solution)/shard_map/ppermute | solution.py:56
  229.8 58.0 %collective-permute-start.27 = (bf16[2,8,24,896]{3,2,1,0:T(8,128)(2,1)}, bf16[2,8,24,896]{3,2,1,0:T(8,128)(2,1)}, u32[]{:S(2)}, u32[]{:S(2)}) collective-permute-start(bf16[2,8,24,896]{3,2,1,0:T(8,128)(2,1)} %bitcast.326), channel_id=1, source_target_pairs={{0,1},{1,0},{2,3},{3,2},{4,5},{5,4},{6,7},{7,6},{8,9},{9,8},{10,11... | collective-permute-start | bytes 2064392 | tf_op jit(solution)/shard_map/ppermute | solution.py:56
  257.4 8.0 %collective-permute-start.14 = (bf16[1,5376]{1,0:T(2,128)(2,1)}, bf16[1,5376]{1,0:T(2,128)(2,1)}, u32[]{:S(2)}, u32[]{:S(2)}) collective-permute-start(bf16[1,5376]{1,0:T(2,128)(2,1)} %constant_dynamic-update-slice_fusion), channel_id=1, source_target_pairs={{0,1},{1,0},{2,3},{3,2},{4,5},{5,4},{6,7},{7,6},{8,9},{9,8},{10,11... | collective-permute-start | bytes 32264 | tf_op jit(solution)/shard_map/ppermute | solution.py:56
  265.5 1.4 collective-permute-start.12
  266.9 3.8 collective-permute-start.15
  270.7 3.8 collective-permute-start.13
  274.5 4.0 collective-permute-start.16
  280.0 4.7 collective-permute-start.17
  281.8 28.1 %collective-permute-start.45 = (bf16[96,768]{1,0:T(8,128)(2,1)}, bf16[96,768]{1,0:T(8,128)(2,1)}, u32[]{:S(2)}, u32[]{:S(2)}) collective-permute-start(bf16[96,768]{1,0:T(8,128)(2,1)} %fusion.100), channel_id=1, source_target_pairs={{0,2},{1,3},{2,0},{3,1},{4,6},{5,7},{6,4},{7,5},{8,10},{9,11},{10,... | collective-permute-start | bytes 442376 | tf_op jit(solution)/shard_map/ppermute | solution.py:56
  284.7 27.0 %collective-permute-start.44 = (bf16[96,768]{1,0:T(8,128)(2,1)}, bf16[96,768]{1,0:T(8,128)(2,1)}, u32[]{:S(2)}, u32[]{:S(2)}) collective-permute-start(bf16[96,768]{1,0:T(8,128)(2,1)} %fusion.100), channel_id=1, source_target_pairs={{0,1},{1,0},{2,3},{3,2},{4,5},{5,4},{6,7},{7,6},{8,9},{9,8},{10,11... | collective-permute-start | bytes 442376 | tf_op jit(solution)/shard_map/ppermute | solution.py:56
  287.8 11.1 %collective-permute-start.18 = (bf16[16,5376]{1,0:T(8,128)(2,1)}, bf16[16,5376]{1,0:T(8,128)(2,1)}, u32[]{:S(2)}, u32[]{:S(2)}) collective-permute-start(bf16[16,5376]{1,0:T(8,128)(2,1)} %concatenate.84), channel_id=1, source_target_pairs={{0,16},{4,20},{8,24},{12,28},{16,0},{20,4},{24,8},{28,12},{1,17},{... | collective-permute-start | bytes 516104 | tf_op jit(solution)/shard_map/ppermute | solution.py:56
  290.9 19.4 %collective-permute-start.28 = (bf16[8,24,896]{2,1,0:T(8,128)(2,1)}, bf16[8,24,896]{2,1,0:T(8,128)(2,1)}, u32[]{:S(2)}, u32[]{:S(2)}) collective-permute-start(bf16[8,24,896]{2,1,0:T(8,128)(2,1)} %dynamic-slice_bitcast_fusion.9), channel_id=1, source_target_pairs={{0,2},{1,3},{2,0},{3,1},{4,6},{5,7},{6,4},{7,5},{8,10},{9,11},{10,... | collective-permute-start | bytes 1032200 | tf_op jit(solution)/shard_map/ppermute | solution.py:56
  298.9 10.9 %collective-permute-start.39 = (bf16[96,768]{1,0:T(8,128)(2,1)}, bf16[96,768]{1,0:T(8,128)(2,1)}, u32[]{:S(2)}, u32[]{:S(2)}) collective-permute-start(bf16[96,768]{1,0:T(8,128)(2,1)} %fusion.101), channel_id=1, source_target_pairs={{0,2},{1,3},{2,0},{3,1},{4,6},{5,7},{6,4},{7,5},{8,10},{9,11},{10,... | collective-permute-start | bytes 442376 | tf_op jit(solution)/shard_map/ppermute | solution.py:56
  309.8 5.0 collective-permute-start.38
  309.9 3.3 collective-permute-start.46
  310.4 4.6 collective-permute-start.40
  311.6 95.8 %collective-permute-start.47 = (bf16[2,2,96,3072]{3,2,0,1:T(8,128)(2,1)}, bf16[2,2,96,3072]{3,2,0,1:T(8,128)(2,1)}, u32[]{:S(2)}, u32[]{:S(2)}) collective-permute-start(bf16[2,2,96,3072]{3,2,0,1:T(8,128)(2,1)} %bitcast.325), channel_id=1, source_target_pairs={{0,4},{4,0},{8,12},{12,8},{16,20},{20,16},{24,28},{28,24},{1,5},{5... | collective-permute-start | bytes 7077896 | tf_op jit(solution)/shard_map/ppermute | solution.py:56
  313.2 56.0 %collective-permute-start.29 = (bf16[2,2,24,896]{3,2,1,0:T(8,128)(2,1)S(1)}, bf16[2,2,24,896]{3,2,1,0:T(8,128)(2,1)S(1)}, u32[]{:S(2)}, u32[]{:S(2)}) collective-permute-start(bf16[2,2,24,896]{3,2,1,0:T(8,128)(2,1)S(1)} %dynamic-slice_bitcast_fusion.13), channel_id=1, source_target_pairs={{0,4},{4,0},{8,12},{12,8},{16,20},{20,16},{24,28},{28,24},{1,5},{5... | collective-permute-start | bytes 516104 | tf_op jit(solution)/shard_map/ppermute | solution.py:56
  314.9 89.0 %collective-permute-start.19 = (bf16[2,8,24,2304]{3,2,1,0:T(8,128)(2,1)}, bf16[2,8,24,2304]{3,2,1,0:T(8,128)(2,1)}, u32[]{:S(2)}, u32[]{:S(2)}) collective-permute-start(bf16[2,8,24,2304]{3,2,1,0:T(8,128)(2,1)} %dynamic-slice_bitcast_fusion), channel_id=1, source_target_pairs={{0,1},{1,0},{2,3},{3,2},{4,5},{5,4},{6,7},{7,6},{8,9},{9,8},{10,11... | collective-permute-start | bytes 5308424 | tf_op jit(solution)/shard_map/ppermute | solution.py:56
  369.3 4.6 collective-permute-start.30
  373.9 5.0 collective-permute-start.31
  379.5 9.4 %collective-permute-start.33 = (bf16[24,896]{1,0:T(8,128)(2,1)}, bf16[24,896]{1,0:T(8,128)(2,1)}, u32[]{:S(2)}, u32[]{:S(2)}) collective-permute-start(bf16[24,896]{1,0:T(8,128)(2,1)} %fusion.104), channel_id=1, source_target_pairs={{0,2},{1,3},{2,0},{3,1},{4,6},{5,7},{6,4},{7,5},{8,10},{9,11},{10,... | collective-permute-start | bytes 129032 | tf_op jit(solution)/shard_map/ppermute | solution.py:56
  388.9 8.0 %collective-permute-start.32 = (bf16[24,896]{1,0:T(8,128)(2,1)}, bf16[24,896]{1,0:T(8,128)(2,1)}, u32[]{:S(2)}, u32[]{:S(2)}) collective-permute-start(bf16[24,896]{1,0:T(8,128)(2,1)} %fusion.104), channel_id=1, source_target_pairs={{0,1},{1,0},{2,3},{3,2},{4,5},{5,4},{6,7},{7,6},{8,9},{9,8},{10,11... | collective-permute-start | bytes 129032 | tf_op jit(solution)/shard_map/ppermute | solution.py:56
  388.9 8.0 %collective-permute-start.34 = (bf16[24,896]{1,0:T(8,128)(2,1)}, bf16[24,896]{1,0:T(8,128)(2,1)}, u32[]{:S(2)}, u32[]{:S(2)}) collective-permute-start(bf16[24,896]{1,0:T(8,128)(2,1)} %collective-permute-done.33), channel_id=1, source_target_pairs={{0,1},{1,0},{2,3},{3,2},{4,5},{5,4},{6,7},{7,6},{8,9},{9,8},{10,11... | collective-permute-start | bytes 129032 | tf_op jit(solution)/shard_map/ppermute | solution.py:56
  406.1 21.6 %collective-permute-start.20 = (bf16[8,24,2304]{2,1,0:T(8,128)(2,1)S(1)}, bf16[8,24,2304]{2,1,0:T(8,128)(2,1)S(1)}, u32[]{:S(2)}, u32[]{:S(2)}) collective-permute-start(bf16[8,24,2304]{2,1,0:T(8,128)(2,1)S(1)} %dynamic-slice_bitcast_fusion.3), channel_id=1, source_target_pairs={{0,2},{1,3},{2,0},{3,1},{4,6},{5,7},{6,4},{7,5},{8,10},{9,11},{10,... | collective-permute-start | bytes 2654216 | tf_op jit(solution)/shard_map/ppermute | solution.py:56
  407.4 28.9 %collective-permute-start.51 = (bf16[2,384,768]{2,1,0:T(8,128)(2,1)S(1)}, bf16[2,384,768]{2,1,0:T(8,128)(2,1)S(1)}, u32[]{:S(2)}, u32[]{:S(2)}) collective-permute-start(bf16[2,384,768]{2,1,0:T(8,128)(2,1)S(1)} %dynamic-slice_bitcast_fusion.1), channel_id=1, source_target_pairs={{0,8},{4,12},{8,0},{12,4},{16,24},{20,28},{24,16},{28,20},{1,9},{5... | collective-permute-start | bytes 3538952 | tf_op jit(solution)/shard_map/ppermute | solution.py:56
  428.0 11.3 %collective-permute-start.21 = (bf16[2,2,24,2304]{3,2,1,0:T(8,128)(2,1)S(1)}, bf16[2,2,24,2304]{3,2,1,0:T(8,128)(2,1)S(1)}, u32[]{:S(2)}, u32[]{:S(2)}) collective-permute-start(bf16[2,2,24,2304]{3,2,1,0:T(8,128)(2,1)S(1)} %dynamic-slice_bitcast_fusion.8), channel_id=1, source_target_pairs={{0,4},{4,0},{8,12},{12,8},{16,20},{20,16},{24,28},{28,24},{1,5},{5... | collective-permute-start | bytes 1327112 | tf_op jit(solution)/shard_map/ppermute | solution.py:56
  429.6 44.6 %collective-permute-start.48 = (bf16[2,96,3072]{2,1,0:T(8,128)(2,1)S(1)}, bf16[2,96,3072]{2,1,0:T(8,128)(2,1)S(1)}, u32[]{:S(2)}, u32[]{:S(2)}) collective-permute-start(bf16[2,96,3072]{2,1,0:T(8,128)(2,1)S(1)} %dynamic-slice_bitcast_fusion.2), channel_id=1, source_target_pairs={{0,8},{4,12},{8,0},{12,4},{16,24},{20,28},{24,16},{28,20},{1,9},{5... | collective-permute-start | bytes 3538952 | tf_op jit(solution)/shard_map/ppermute | solution.py:56
  436.7 75.2 %collective-permute-start.52 = (bf16[384,768]{1,0:T(8,128)(2,1)S(1)}, bf16[384,768]{1,0:T(8,128)(2,1)S(1)}, u32[]{:S(2)}, u32[]{:S(2)}) collective-permute-start(bf16[384,768]{1,0:T(8,128)(2,1)S(1)} %dynamic-slice_bitcast_fusion.4), channel_id=1, source_target_pairs={{0,16},{4,20},{8,24},{12,28},{16,0},{20,4},{24,8},{28,12},{1,17},{... | collective-permute-start | bytes 1769480 | tf_op jit(solution)/shard_map/ppermute | solution.py:56
  439.5 38.2 %collective-permute-start.22 = (bf16[2,24,2304]{2,1,0:T(8,128)(2,1)S(1)}, bf16[2,24,2304]{2,1,0:T(8,128)(2,1)S(1)}, u32[]{:S(2)}, u32[]{:S(2)}) collective-permute-start(bf16[2,24,2304]{2,1,0:T(8,128)(2,1)S(1)} %dynamic-slice_bitcast_fusion.12), channel_id=1, source_target_pairs={{0,8},{4,12},{8,0},{12,4},{16,24},{20,28},{24,16},{28,20},{1,9},{5... | collective-permute-start | bytes 663560 | tf_op jit(solution)/shard_map/ppermute | solution.py:56
  477.8 19.9 %collective-permute-start.23 = (bf16[24,2304]{1,0:T(8,128)(2,1)S(1)}, bf16[24,2304]{1,0:T(8,128)(2,1)S(1)}, u32[]{:S(2)}, u32[]{:S(2)}) collective-permute-start(bf16[24,2304]{1,0:T(8,128)(2,1)S(1)} %dynamic-slice_bitcast_fusion.16), channel_id=1, source_target_pairs={{0,16},{4,20},{8,24},{12,28},{16,0},{20,4},{24,8},{28,12},{1,17},{... | collective-permute-start | bytes 331784 | tf_op jit(solution)/shard_map/ppermute | solution.py:56
  478.2 32.0 %collective-permute-start.49 = (bf16[96,3072]{1,0:T(8,128)(2,1)S(1)}, bf16[96,3072]{1,0:T(8,128)(2,1)S(1)}, u32[]{:S(2)}, u32[]{:S(2)}) collective-permute-start(bf16[96,3072]{1,0:T(8,128)(2,1)S(1)} %dynamic-slice_bitcast_fusion.5), channel_id=1, source_target_pairs={{0,16},{4,20},{8,24},{12,28},{16,0},{20,4},{24,8},{28,12},{1,17},{... | collective-permute-start | bytes 1769480 | tf_op jit(solution)/shard_map/ppermute | solution.py:56
  497.7 13.6 %collective-permute-start.25 = (bf16[24,2304]{1,0:T(8,128)(2,1)S(1)}, bf16[24,2304]{1,0:T(8,128)(2,1)S(1)}, u32[]{:S(2)}, u32[]{:S(2)}) collective-permute-start(bf16[24,2304]{1,0:T(8,128)(2,1)S(1)} %fusion.102), channel_id=1, source_target_pairs={{0,2},{1,3},{2,0},{3,1},{4,6},{5,7},{6,4},{7,5},{8,10},{9,11},{10,... | collective-permute-start | bytes 331784 | tf_op jit(solution)/shard_map/ppermute | solution.py:56
  511.3 1.7 collective-permute-start.24
  511.4 1.6 collective-permute-start.26
  (74 other events, 391.3 us)
